TPU v7x, 32 devices: a whole 2x2x4 slice. The times are simulated.
32 devices in a mesh: rep: 8 (over z, x), exp: 4 (over y, core).
Axes of the slice: x: 2, y: 2, z: 4, core: 2. Of those that a mesh axis runs over, the one named last changes fastest.
Arguments:
- tokens: bfloat16 [4096, 2048], P(('rep', 'exp')), may hold values from -6 to 6
- expert_ids: int32 [4096, 1], P(('rep', 'exp')), may hold values from 0 to 3; in each aligned block of 128 rows (0 to 127, 128 to 255, ...) at most 32 rows name the same one
- gate_prob: float32 [4096], P(('rep', 'exp')), may hold values from 0.05 to 1
- cotangent: bfloat16 [4096, 2048], P(('rep', 'exp')), may hold values from -6 to 6
- w_gate: bfloat16 [8, 2048, 4096], P('rep', None, 'exp'), may hold values from -0.125 to 0.125
- w_up: bfloat16 [8, 2048, 4096], P('rep', None, 'exp'), may hold values from -0.125 to 0.125
- w_down: bfloat16 [8, 4096, 2048], P('rep', 'exp'), may hold values from -0.1875 to 0.1875
- touched: int32 [8, 256], P('rep', 'exp'), may hold values 0 or 1
Outputs:
- mixed: bfloat16 [4096, 2048], P(('rep', 'exp'))
- averaged: bfloat16 [4096, 6144], P('exp', 'rep')
Inputs may be any that keep to these rules, and one draw needn't show every extreme that they name: `expert_ids`: the rows of one device name each of the 4 window experts exactly 32 times.
All inputs are finite; a program needn't handle non-finite values. No bound on the sum of `touched` on one device may be relied on, other than what follows from the above.
Results may differ from a plain program's by a relative error of at most 0.018.
Values may be sent and summed in bfloat16 or wider, within the bound.
A program may use at most 128 MiB of HBM per device.

v0:
```python
import jax
import jax.numpy as jnp
from jax import lax
from jax.sharding import PartitionSpec as P

EW = 4
TILE = 16


def swish_slope(h):
    s = jax.nn.sigmoid(h)
    return s * (1.0 + h * (1.0 - s))


def body(tokens, expert_ids, gate_prob, cotangent, w_gate, w_up, w_down, touched):
    rows = tokens.shape[0]
    width = tokens.shape[1]
    n_exp = lax.axis_size("exp")
    n_rep = lax.axis_size("rep")
    shards = n_exp // EW
    cap = rows // EW
    onehot = (expert_ids == jnp.arange(EW)[None, :]).astype(jnp.float32)
    lower = (
        lax.broadcasted_iota(jnp.int32, (rows, rows), 0)
        > lax.broadcasted_iota(jnp.int32, (rows, rows), 1)
    ).astype(jnp.float32)
    earlier = jnp.dot(lower, onehot, precision=lax.Precision.HIGHEST)
    slot_of = jnp.sum(onehot * earlier, axis=1).astype(jnp.int32)
    target = expert_ids[:, 0] * cap + slot_of
    placer = (target[None, :] == jnp.arange(EW * cap)[:, None]).astype(jnp.bfloat16)
    dy = (gate_prob[:, None] * cotangent.astype(jnp.float32)).astype(jnp.bfloat16)
    x_buf = (
        jnp.dot(placer, tokens, preferred_element_type=jnp.float32)
        .astype(jnp.bfloat16)
        .reshape(EW, cap, width)
    )
    d_buf = (
        jnp.dot(placer, dy, preferred_element_type=jnp.float32)
        .astype(jnp.bfloat16)
        .reshape(EW, cap, width)
    )
    x_recv, d_recv = (
        lax.all_to_all(
            jnp.repeat(x_buf, shards, axis=0), "exp", split_axis=0, concat_axis=0, tiled=True
        ),
        lax.all_to_all(
            jnp.repeat(d_buf, shards, axis=0), "exp", split_axis=0, concat_axis=0, tiled=True
        ),
    )
    x_rows = x_recv.reshape(n_exp * cap, width)
    d_rows = d_recv.reshape(n_exp * cap, width)
    wg = w_gate[0]
    wu = w_up[0]
    wd = w_down[0]
    h = jnp.dot(x_rows, wg, preferred_element_type=jnp.float32)
    u = jnp.dot(x_rows, wu, preferred_element_type=jnp.float32)
    act = (h * jax.nn.sigmoid(h) * u).astype(jnp.bfloat16)
    partial_out = jnp.dot(act, wd, preferred_element_type=jnp.float32).astype(jnp.bfloat16)
    returned = lax.all_to_all(
        partial_out.reshape(n_exp, cap, width), "exp", split_axis=0, concat_axis=0, tiled=True
    )
    summed = returned.astype(jnp.float32).reshape(EW, shards, cap, width).sum(axis=1)
    row_out = jnp.take(summed.reshape(EW * cap, width), target, axis=0)
    mixed = (gate_prob[:, None] * row_out).astype(jnp.bfloat16)
    grad_a = lax.dot_general(
        d_rows, wd, (((1,), (1,)), ((), ())), preferred_element_type=jnp.float32
    )
    d_down = lax.dot_general(
        act, d_rows, (((0,), (0,)), ((), ())), preferred_element_type=jnp.float32
    )
    d_h = (grad_a * u * swish_slope(h)).astype(jnp.bfloat16)
    d_u = (grad_a * h * jax.nn.sigmoid(h)).astype(jnp.bfloat16)
    d_gate = lax.dot_general(
        d_h, x_rows, (((0,), (0,)), ((), ())), preferred_element_type=jnp.float32
    )
    d_upper = lax.dot_general(
        d_u, x_rows, (((0,), (0,)), ((), ())), preferred_element_type=jnp.float32
    )
    delta = jnp.concatenate([d_gate, d_upper, d_down], axis=1)
    weight_rows = jnp.repeat(touched[0].astype(jnp.float32), TILE)
    masked = delta * weight_rows[:, None]
    columns = delta.shape[1] // n_rep
    total = lax.psum(masked.astype(jnp.bfloat16), "rep").astype(jnp.float32)
    share = lax.dynamic_slice_in_dim(total, lax.axis_index("rep") * columns, columns, 1)
    averaged = (share / n_rep).astype(jnp.bfloat16)
    return (mixed, averaged)


def solution(mesh):
    return jax.shard_map(
        body,
        mesh=mesh,
        in_specs=(
            P(("rep", "exp"), None),
            P(("rep", "exp"), None),
            P(("rep", "exp")),
            P(("rep", "exp"), None),
            P("rep", None, "exp"),
            P("rep", None, "exp"),
            P("rep", "exp", None),
            P("rep", "exp"),
        ),
        out_specs=(P(("rep", "exp"), None), P("exp", "rep")),
        check_vma=False,
    )
```

profile of v0, /device:TPU:0, one launch (start us, length us, event | category | flops | bytes accessed | tf_op | source)
XLA Modules:
  0.0 457.6 jit_solution(14118961964658739959)
XLA Ops:
  7.2 0.0 copy-start
  7.2 0.9 fusion.12
  8.1 0.7 multiply_add_fusion
  8.7 0.0 copy-done
  8.7 1.1 convolution_convert_fusion.1
  9.8 4.2 all-to-all-start
  14.1 0.7 convert_bitcast_fusion
  14.7 0.1 broadcast_in_dim.20
  14.8 0.1 mul.86
  14.9 2.2 convolution_convert_fusion
  17.1 5.8 %all-to-all-done = bf16[4,32,2048]{2,1,0:T(8,128)(2,1)S(1)} async-done(((bf16[4,32,2048]{2,1,0:T(8,128)(2,1)}), bf16[4,32,2048]{2,1,0:T(8,128)(2,1)S(1)}, u32[]{:S(2)}, u32[]{:S(2)}) %all-to-all-start) | async-done | bytes 524320 | tf_op jit(solution)/shard_map/all_to_all | solution.py:43
  22.9 3.5 all-to-all-start.2
  26.4 0.0 all-reduce.2.cloned.1.call-start
  26.4 0.0 copy-start.4
  26.5 3.1 fusion.7
  29.5 0.4 copy-done.4
  29.9 0.8 multiply_convert_fusion.6
  30.7 4.5 all-to-all-done.2
  35.2 3.7 fusion.1
  38.9 1.3 fusion.15
  40.2 1.3 fusion.14
  41.6 1.3 fusion.23
  42.9 6.3 %fusion = bf16[1024,6144]{1,0:T(8,128)(2,1)} fusion(f32[1024,2048]{1,0:T(8,128)S(1)} %fusion.23, f32[1024,2048]{1,0:T(8,128)S(1)} %fusion.15, f32[1024,2048]{1,0:T(8,128)S(1)} %fusion.14, f32[1024]{0:T(1024)S(1)} %mul.86), kind=kLoop, calls=%fused_computation.2 | loop fusion | flops 25165824 | bytes 37752832 | tf_op jit(solution)/shard_map/convert_element_type | solution.py:83
  49.2 0.0 all-reduce.2.cloned.1.call-update
  49.2 0.0 copy-start.3
  49.2 3.7 fusion.9
  52.9 3.5 all-to-all-start.1
  56.5 0.0 copy-done.3
  56.5 8.8 %all-to-all-done.1 = bf16[4,32,2048]{2,1,0:T(8,128)(2,1)S(1)} async-done(((bf16[4,32,2048]{2,1,0:T(8,128)(2,1)}), bf16[4,32,2048]{2,1,0:T(8,128)(2,1)S(1)}, u32[]{:S(2)}, u32[]{:S(2)}) %all-to-all-start.1) | async-done | bytes 524320 | tf_op jit(solution)/shard_map/all_to_all | solution.py:59
  65.3 0.1 bitcast_convert_fusion
  65.4 0.0 copy-start.2
  65.4 0.0 copy-start.1
  65.4 1.0 gather_fusion
  66.4 0.0 copy-done.2
  66.4 1.0 multiply_convert_fusion.2
  67.4 380.5 %all-reduce.2.cloned.1.call-done = bf16[1024,6144]{1,0:T(8,128)(2,1)} async-done(((bf16[1024,6144]{1,0:T(8,128)(2,1)}), bf16[1024,6144]{1,0:T(8,128)(2,1)}) %all-reduce.2.cloned.1.call-update) | async-done | bytes 12582928 | tf_op jit(solution)/shard_map/psum | solution.py:83
  447.9 2.8 multiply_convert_fusion
  450.8 0.0 copy-done.1
  (2 shorter events, 0.0 us)
Async XLA Ops:
  7.2 1.6 copy-start
  9.8 13.1 %all-to-all-start = ((bf16[4,32,2048]{2,1,0:T(8,128)(2,1)}), bf16[4,32,2048]{2,1,0:T(8,128)(2,1)S(1)}, u32[]{:S(2)}, u32[]{:S(2)}) async-start(bf16[4,32,2048]{2,1,0:T(8,128)(2,1)} %bitcast.3), calls=%async_computation | async-start | bytes 1048576 | tf_op jit(solution)/shard_map/all_to_all | solution.py:43
  22.9 12.3 %all-to-all-start.2 = ((bf16[4,32,2048]{2,1,0:T(8,128)(2,1)}), bf16[4,32,2048]{2,1,0:T(8,128)(2,1)S(1)}, u32[]{:S(2)}, u32[]{:S(2)}) async-start(bf16[4,32,2048]{2,1,0:T(8,128)(2,1)} %bitcast.11), calls=%async_computation.2 | async-start | bytes 1048576 | tf_op jit(solution)/shard_map/all_to_all | solution.py:46
  26.4 421.5 %all-reduce.2.cloned.1.call-start = ((), (), s32[]{:S(2)}) async-start(), calls=%async_computation.3 | async-start | bytes 25165824 | tf_op jit(solution)/shard_map/psum | solution.py:83
  26.4 3.5 copy-start.4
  49.2 7.3 %copy-start.3 = (s32[128,1]{0,1:T(1,128)S(1)}, s32[128,1]{0,1:T(1,128)}, u32[]{:S(2)}) copy-start(s32[128,1]{0,1:T(1,128)} %param.9) | copy-start | bytes 1540
  52.9 12.3 %all-to-all-start.1 = ((bf16[4,32,2048]{2,1,0:T(8,128)(2,1)}), bf16[4,32,2048]{2,1,0:T(8,128)(2,1)S(1)}, u32[]{:S(2)}, u32[]{:S(2)}) async-start(bf16[4,32,2048]{2,1,0:T(8,128)(2,1)} %bitcast.8), calls=%async_computation.1 | async-start | bytes 1048576 | tf_op jit(solution)/shard_map/all_to_all | solution.py:59
  65.4 1.0 copy-start.2
  65.4 385.3 %copy-start.1 = (bf16[128,2048]{1,0:T(8,128)(2,1)S(1)}, bf16[128,2048]{1,0:T(8,128)(2,1)}, u32[]{:S(2)}) copy-start(bf16[128,2048]{1,0:T(8,128)(2,1)} %param.8) | copy-start | bytes 1572868
Sparse Core Ops, SparseCore 0:
  49.3 398.5 all-reduce.1
where the time goes:
time: 458 us
  waiting for transfers between devices  400 us (87%)
  matrix products  19.4 us (4%)
  between operations  14.2 us (3%)
  other arithmetic  11.6 us (3%)
  starting transfers between devices  11.3 us (2%)
    psum x1, waiting for transfers between devices, body(): total = lax.psum(masked.astype(jnp.bfloat16), 'rep').astype(jnp.float32)  381 us
  transfers between devices with their start and end apart: 4, of which 4 were waited for; matrix products, arithmetic and copies ran while one was open for 3% of the time, Pallas kernels for 0%

commit v1 on v0

v1 whole, which is shorter than its diff:
```python
import functools
import math

import jax
import jax.numpy as jnp
from jax import lax
from jax.experimental import pallas as pl
from jax.experimental.pallas import tpu as pltpu
from jax.sharding import PartitionSpec as P

EW = 4
TILE = 16
PIECES = 8
AHEAD = 2
B_LAG = 2
F32 = jnp.float32
BF16 = jnp.bfloat16


def swish_slope(h):
    s = jax.nn.sigmoid(h)
    return s * (1.0 + h * (1.0 - s))


def reduce_kernel(
    n, l_ref, r_ref, out_ref, xsend, xrecv, up, down, own_b, up_b, down_b, xs_b, xr_b,
    xs_sem, xr_sem, us_sem, ur_sem, ds_sem, dr_sem,
    bus_sem, bur_sem, bds_sem, bdr_sem, bx_sem,
):
    na = PIECES - 1
    n_rep = 2 * n
    tpc = xsend.shape[2]
    tw = xsend.shape[4]
    pr = xsend.shape[3]
    tpw = r_ref.shape[0] // 2
    rep = lax.axis_index("rep")
    z = rep // 2
    x = rep % 2
    peer = {"rep": rep + 1 - 2 * x}
    above = {"rep": jnp.minimum(rep + 2, n_rep - 1)}
    below = {"rep": jnp.maximum(rep - 2, 0)}
    last = n - 1
    b_lag = B_LAG if B_LAG * last < na + last else 1

    def part(p, r, j):
        t = r * tpc + j
        mat = t // tpw
        src = t % tpw + jnp.where(mat == 2, tpw, 0)
        return jnp.dot(l_ref[mat, p], r_ref[src], preferred_element_type=F32)

    def remote(src, dst, send, recv, dev):
        return pltpu.make_async_remote_copy(
            src_ref=src, dst_ref=dst, send_sem=send, recv_sem=recv,
            device_id=dev, device_id_type=pl.DeviceIdType.MESH,
        )

    def x_copy(p):
        return remote(xsend.at[p], xrecv.at[p], xs_sem.at[p], xr_sem.at[p], peer)

    def up_copy(src, p, d):
        return remote(src.at[p, d], up.at[p, d], us_sem.at[p, d], ur_sem.at[p, d], above)

    def down_copy(src, p, d):
        return remote(src.at[p, d], down.at[p, d], ds_sem.at[p, d], dr_sem.at[p, d], below)

    def upb_copy(src, d):
        return remote(src.at[d], up_b.at[d], bus_sem.at[d], bur_sem.at[d], above)

    def downb_copy(src, d):
        return remote(src.at[d], down_b.at[d], bds_sem.at[d], bdr_sem.at[d], below)

    def xb_copy():
        return remote(xs_b, xr_b, bx_sem.at[0], bx_sem.at[1], peer)

    barrier = pltpu.get_barrier_semaphore()
    mesh_id = pl.DeviceIdType.MESH
    pl.semaphore_signal(barrier, inc=1, device_id=peer, device_id_type=mesh_id)

    @pl.when(z < last)
    def _():
        pl.semaphore_signal(barrier, inc=1, device_id=above, device_id_type=mesh_id)

    @pl.when(z > 0)
    def _():
        pl.semaphore_signal(barrier, inc=1, device_id=below, device_id_type=mesh_id)

    pl.semaphore_wait(barrier, 1 + jnp.where(z < last, 1, 0) + jnp.where(z > 0, 1, 0))

    def send_x(p):
        def one(d, c):
            for j in range(tpc):
                xsend[p, d, j] = part(p, 2 * d + 1 - x, j).astype(BF16)
            return c

        lax.fori_loop(0, n, one, 0)
        x_copy(p).start()

    send_x(0)

    def build_b(r, c):
        for j in range(tpc):
            own_b[r // 2, r % 2, j] = part(na, r, j).astype(BF16)
        return c

    lax.fori_loop(0, n_rep, build_b, 0)

    @pl.when(z == 0)
    def _():
        for d in range(last, 0, -1):
            upb_copy(own_b, d).start()

    @pl.when(z == last)
    def _():
        for d in range(last):
            downb_copy(own_b, d).start()

    for p in range(1, AHEAD):
        send_x(p)

    def add_into(dst, src):
        for j in range(tpc):
            dst[j] = (dst[j].astype(F32) + src[j].astype(F32)).astype(BF16)

    def step(i, carry):
        @pl.when(i + AHEAD < na)
        def _():
            send_x(i + AHEAD)

        @pl.when(i < na)
        def _():
            x_copy(i).wait_recv()

            def one(d, c):
                for j in range(tpc):
                    xrecv[i, d, j] = (part(i, 2 * d + x, j) + xrecv[i, d, j].astype(F32)).astype(BF16)
                return c

            lax.fori_loop(0, n, one, 0)

            @pl.when(z == 0)
            def _():
                for d in range(last, 0, -1):
                    up_copy(xrecv, i, d).start()

            @pl.when(z == last)
            def _():
                for d in range(last):
                    down_copy(xrecv, i, d).start()

        q = i - z

        @pl.when((z > 0) & (z < last) & (q >= 0) & (q < na))
        def _():
            for d in range(last, 1, -1):
                @pl.when(d > z)
                def _():
                    up_copy(up, q, d).wait_recv()
                    add_into(up.at[q, d], xrecv.at[q, d])
                    up_copy(up, q, d).start()

        w = i - (last - z)

        @pl.when((z > 0) & (z < last) & (w >= 0) & (w < na))
        def _():
            for d in range(last - 1):
                @pl.when(d < z)
                def _():
                    down_copy(down, w, d).wait_recv()
                    add_into(down.at[w, d], xrecv.at[w, d])
                    down_copy(down, w, d).start()

        f = i - last

        @pl.when((f >= 0) & (f < na))
        def _():
            @pl.when(z > 0)
            def _():
                up_copy(up, f, z).wait_recv()

            @pl.when(z < last)
            def _():
                down_copy(down, f, z).wait_recv()

            for j in range(tpc):
                total = xrecv[f, z, j].astype(F32)
                total += jnp.where(z > 0, up[f, z, j].astype(F32), 0.0)
                total += jnp.where(z < last, down[f, z, j].astype(F32), 0.0)
                out_ref[f, :, j * tw:(j + 1) * tw] = (total / n_rep).astype(BF16)

        @pl.when((z > 0) & (z < last) & (i == b_lag * z))
        def _():
            for d in range(last, 1, -1):
                @pl.when(d > z)
                def _():
                    upb_copy(up_b, d).wait_recv()
                    for k in range(2):
                        add_into(up_b.at[d, k], own_b.at[d, k])
                    upb_copy(up_b, d).start()

        @pl.when((z > 0) & (z < last) & (i == b_lag * (last - z)))
        def _():
            for d in range(last - 1):
                @pl.when(d < z)
                def _():
                    downb_copy(down_b, d).wait_recv()
                    for k in range(2):
                        add_into(down_b.at[d, k], own_b.at[d, k])
                    downb_copy(down_b, d).start()

        @pl.when(i == b_lag * last)
        def _():
            @pl.when(z > 0)
            def _():
                upb_copy(up_b, z).wait_recv()

            @pl.when(z < last)
            def _():
                downb_copy(down_b, z).wait_recv()

            for k in range(2):
                for j in range(tpc):
                    total = own_b[z, k, j].astype(F32)
                    total += jnp.where(z > 0, up_b[z, k, j].astype(F32), 0.0)
                    total += jnp.where(z < last, down_b[z, k, j].astype(F32), 0.0)
                    own_b[z, k, j] = total.astype(BF16)
            for j in range(tpc):
                xs_b[j] = own_b[z, 1 - x, j]
            xb_copy().start()

        return carry

    lax.fori_loop(0, na + last, step, 0)

    xb_copy().wait_recv()
    for j in range(tpc):
        total = own_b[z, x, j].astype(F32) + xr_b[j].astype(F32)
        out_ref[na, :, j * tw:(j + 1) * tw] = (total / n_rep).astype(BF16)
    xb_copy().wait_send()

    def drain(i, carry):
        x_copy(i).wait_send()

        @pl.when(z < last)
        def _():
            for d in range(1, n):
                @pl.when(d > z)
                def _():
                    up_copy(up, i, d).wait_send()

        @pl.when(z > 0)
        def _():
            for d in range(last):
                @pl.when(d < z)
                def _():
                    down_copy(down, i, d).wait_send()

        return carry

    lax.fori_loop(0, na, drain, 0)

    @pl.when(z < last)
    def _():
        for d in range(1, n):
            @pl.when(d > z)
            def _():
                upb_copy(up_b, d).wait_send()

    @pl.when(z > 0)
    def _():
        for d in range(last):
            @pl.when(d < z)
            def _():
                downb_copy(down_b, d).wait_send()


def reduce_deltas(left, right, n_rep, columns):
    n = n_rep // 2
    pr, depth = left.shape[2:]
    tw = right.shape[2]
    tpc = columns // tw
    na = PIECES - 1
    chunk = (tpc, pr, tw)
    dma = pltpu.SemaphoreType.DMA
    vmem = pl.BlockSpec(memory_space=pltpu.VMEM)
    out = pl.pallas_call(
        functools.partial(reduce_kernel, n),
        out_shape=jax.ShapeDtypeStruct((PIECES, pr, columns), BF16),
        in_specs=[vmem] * 2,
        out_specs=vmem,
        scratch_shapes=[
            pltpu.VMEM((na, n) + chunk, BF16),
            pltpu.VMEM((na, n) + chunk, BF16),
            pltpu.VMEM((na, n) + chunk, BF16),
            pltpu.VMEM((na, n) + chunk, BF16),
            pltpu.VMEM((n, 2) + chunk, BF16),
            pltpu.VMEM((n, 2) + chunk, BF16),
            pltpu.VMEM((n, 2) + chunk, BF16),
            pltpu.VMEM(chunk, BF16),
            pltpu.VMEM(chunk, BF16),
            dma((na,)),
            dma((na,)),
            dma((na, n)),
            dma((na, n)),
            dma((na, n)),
            dma((na, n)),
            dma((n,)),
            dma((n,)),
            dma((n,)),
            dma((n,)),
            dma((2,)),
        ],
        compiler_params=pltpu.CompilerParams(
            collective_id=0, has_side_effects=True, vmem_limit_bytes=56 * 2**20
        ),
        cost_estimate=pl.CostEstimate(
            flops=2 * 3 * PIECES * pr * depth * columns * n_rep // 3,
            bytes_accessed=8 * 2**20, transcendentals=0,
        ),
    )(left, right)
    return out.reshape(PIECES * pr, columns)


def body(tokens, expert_ids, gate_prob, cotangent, w_gate, w_up, w_down, touched):
    rows = tokens.shape[0]
    width = tokens.shape[1]
    n_exp = lax.axis_size("exp")
    n_rep = lax.axis_size("rep")
    shards = n_exp // EW
    cap = rows // EW
    onehot = (expert_ids == jnp.arange(EW)[None, :]).astype(jnp.float32)
    lower = (
        lax.broadcasted_iota(jnp.int32, (rows, rows), 0)
        > lax.broadcasted_iota(jnp.int32, (rows, rows), 1)
    ).astype(jnp.float32)
    earlier = jnp.dot(lower, onehot, precision=lax.Precision.HIGHEST)
    slot_of = jnp.sum(onehot * earlier, axis=1).astype(jnp.int32)
    target = expert_ids[:, 0] * cap + slot_of
    placer = (target[None, :] == jnp.arange(EW * cap)[:, None]).astype(jnp.bfloat16)
    dy = (gate_prob[:, None] * cotangent.astype(jnp.float32)).astype(jnp.bfloat16)
    both = jnp.dot(
        placer, jnp.concatenate([tokens, dy], axis=1), preferred_element_type=jnp.float32
    ).astype(jnp.bfloat16).reshape(EW, cap, 2 * width)
    recv = lax.all_to_all(
        jnp.repeat(both, shards, axis=0), "exp", split_axis=0, concat_axis=0, tiled=True
    ).reshape(n_exp * cap, 2 * width)
    x_rows = recv[:, :width]
    d_rows = recv[:, width:]
    wg = w_gate[0]
    wu = w_up[0]
    wd = w_down[0]
    h = jnp.dot(x_rows, wg, preferred_element_type=jnp.float32)
    u = jnp.dot(x_rows, wu, preferred_element_type=jnp.float32)
    act = (h * jax.nn.sigmoid(h) * u).astype(jnp.bfloat16)
    partial_out = jnp.dot(act, wd, preferred_element_type=jnp.float32).astype(jnp.bfloat16)
    returned = lax.all_to_all(
        partial_out.reshape(n_exp, cap, width), "exp", split_axis=0, concat_axis=0, tiled=True
    )
    summed = returned.astype(jnp.float32).reshape(EW, shards, cap, width).sum(axis=1)
    row_out = jnp.take(summed.reshape(EW * cap, width), target, axis=0)
    mixed = (gate_prob[:, None] * row_out).astype(jnp.bfloat16)
    grad_a = lax.dot_general(
        d_rows, wd, (((1,), (1,)), ((), ())), preferred_element_type=jnp.float32
    )
    d_h = (grad_a * u * swish_slope(h)).astype(jnp.bfloat16)
    d_u = (grad_a * h * jax.nn.sigmoid(h)).astype(jnp.bfloat16)
    hidden = d_h.shape[1]
    columns = 3 * width // n_rep
    tw = math.gcd(columns, width)
    mask = jnp.repeat(touched[0], TILE).astype(jnp.bfloat16)
    left = (jnp.stack([d_h, d_u, act]) * mask[None, None, :]).transpose(0, 2, 1)
    left = left.reshape(3, PIECES, hidden // PIECES, left.shape[2])
    right = recv.reshape(recv.shape[0], 2 * width // tw, tw).transpose(1, 0, 2)
    averaged = reduce_deltas(left, right, n_rep, columns)
    return (mixed, averaged)


def solution(mesh):
    return jax.shard_map(
        body,
        mesh=mesh,
        in_specs=(
            P(("rep", "exp"), None),
            P(("rep", "exp"), None),
            P(("rep", "exp")),
            P(("rep", "exp"), None),
            P("rep", None, "exp"),
            P("rep", None, "exp"),
            P("rep", "exp", None),
            P("rep", "exp"),
        ),
        out_specs=(P(("rep", "exp"), None), P("exp", "rep")),
        check_vma=False,
    )
```

time: 458 us -> 194 us (0.42)
  waiting for transfers between devices: 400 us -> 14.3 us
  Pallas kernels: 0 us -> 150 us
  between operations: 14.2 us -> 0.78 us
  matrix products: 19.4 us -> 10.5 us
  other arithmetic: 11.6 us -> 3.1 us
  local copies, waits for them, and re-layouts: 1.54 us -> 7.77 us
    psum x1 -> x0, waiting for transfers between devices: 381 us -> none  [body(): total = lax.psum(masked.astype(jnp.bfloat16), 'rep').astype(jnp.float32)]
    pallas_call x0 -> x1, Pallas kernels: none -> 150 us  [reduce_deltas(): pl.pallas_call(functools.partial(reduce_kernel, n), out_shape=jax.ShapeDt...]
    all_to_all x1, waiting for transfers between devices: 8.76 us -> 0.01 us  [body(): lax.all_to_all(partial_out.reshape(n_exp, cap, width), 'exp', split_axis=...]
    convert_element_type x3 -> x2, other arithmetic: 9.82 us -> 1.2 us  [the longest x1 1.2 us: body(): (gate_prob[:, None] * cotangent.astype(jnp.float32)).astype(jnp.bfloat16)]
    dot_general x5 -> x1, matrix products: 7.24 us -> 2.44 us  [body(): jnp.dot(placer, jnp.concatenate([tokens, dy], axis=1), preferred_element_...]
    all_to_all x2 -> x1, waiting for transfers between devices: 10.3 us -> 14.3 us  [body(): lax.all_to_all(jnp.repeat(both, shards, axis=0), 'exp', split_axis=0, con...]
  transfers between devices with their start and end apart: 4 -> 2, of which waited for: 4 -> 1; matrix products, arithmetic and copies ran while one was open for 3% -> 2% of each run, Pallas kernels for 0% -> 77%
where the time goes in v1:
time: 194 us
  Pallas kernels  150 us (77%)
  waiting for transfers between devices  14.3 us (7%)
  matrix products  10.5 us (5%)
  local copies, waits for them, and re-layouts  7.77 us (4%)
  starting transfers between devices  7.71 us (4%)
  other arithmetic  3.1 us (2%)
    pallas_call x1, Pallas kernels, reduce_deltas(): pl.pallas_call(functools.partial(reduce_kernel, n), out_shape=jax.ShapeDt...  150 us
    all_to_all x1, waiting for transfers between devices, body(): lax.all_to_all(jnp.repeat(both, shards, axis=0), 'exp', split_axis=0, con...  14.3 us
    all_to_all x1, starting transfers between devices, body(): lax.all_to_all(jnp.repeat(both, shards, axis=0), 'exp', split_axis=0, con...  4.24 us
    unnamed x14, local copies, waits for them, and re-layouts  4.17 us
  transfers between devices with their start and end apart: 2, of which 1 were waited for; matrix products, arithmetic and copies ran while one was open for 2% of the time, Pallas kernels for 77%

profile of v1, /device:TPU:0, one launch (start us, length us, event | category | flops | bytes accessed | tf_op | source)
XLA Modules:
  0.0 193.9 jit_solution(7977660283497593842)
XLA Ops:
  0.6 0.0 copy-start.3
  0.6 0.0 copy-start.5
  0.7 0.9 fusion.11
  1.5 0.7 multiply_add_fusion
  2.2 1.2 multiply_convert_fusion.1
  3.4 2.4 %convolution_convert_fusion = bf16[128,4096]{1,0:T(8,128)(2,1)} fusion(bf16[128,2048]{1,0:T(8,128)(2,1)S(1)} %multiply_convert_fusion.1, bf16[128,2048]{1,0:T(8,128)(2,1)} %param.8, s32[128]{0:T(128)S(1)} %multiply_add_fusion), kind=kOutput, calls=%fused_computation.1 | convolution fusion | flops 136855552 | bytes 2097664 | tf_op jit(solution)/shard_map/dot_general | solution.py:340
  5.9 4.2 %all-to-all-start = ((bf16[4,32,4096]{2,1,0:T(8,128)(2,1)}), bf16[4,32,4096]{2,1,0:T(8,128)(2,1)S(1)}, u32[]{:S(2)}, u32[]{:S(2)}) async-start(bf16[4,32,4096]{2,1,0:T(8,128)(2,1)} %bitcast.3), calls=%async_computation | async-start | bytes 2097152 | tf_op jit(solution)/shard_map/all_to_all | solution.py:343
  10.1 0.0 copy-done.5
  10.1 0.1 broadcast_in_dim.21
  10.2 0.1 convert_element_type.72
  10.3 0.0 copy-done.3
  10.3 14.3 %all-to-all-done = bf16[4,32,4096]{2,1,0:T(8,128)(2,1)S(1)} async-done(((bf16[4,32,4096]{2,1,0:T(8,128)(2,1)}), bf16[4,32,4096]{2,1,0:T(8,128)(2,1)S(1)}, u32[]{:S(2)}, u32[]{:S(2)}) %all-to-all-start) | async-done | bytes 1048608 | tf_op jit(solution)/shard_map/all_to_all | solution.py:343
  24.6 0.0 copy-start.1
  24.6 0.0 copy-start.4
  24.6 3.8 %fusion = f32[128,1024]{1,0:T(8,128)S(1)} fusion(bf16[1,1024,2048]{2,1,0:T(8,128)(2,1)} %param.14, bf16[128,4096]{1,0:T(8,128)(2,1)S(1)} %bitcast.49), kind=kOutput, calls=%fused_computation.2 | convolution fusion | flops 536870912 | bytes 5242880 | tf_op jit(solution)/shard_map/dot_general | solution.py:361
  28.4 0.0 copy-done.1
  28.4 0.7 fusion.4
  29.2 0.1 copy-done.4
  29.3 0.0 copy-start
  29.3 1.0 fusion.20
  30.4 1.1 copy-done
  31.5 1.5 fusion.8
  33.0 3.5 %all-to-all-start.1 = ((bf16[4,32,2048]{2,1,0:T(8,128)(2,1)}), bf16[4,32,2048]{2,1,0:T(8,128)(2,1)S(1)}, u32[]{:S(2)}, u32[]{:S(2)}) async-start(bf16[4,32,2048]{2,1,0:T(8,128)(2,1)} %bitcast.8), calls=%async_computation.1 | async-start | bytes 1048576 | tf_op jit(solution)/shard_map/all_to_all | solution.py:355
  36.5 0.1 fusion.15
  36.6 1.2 copy.11
  37.8 0.2 copy.13
  38.0 1.3 copy.15
  39.3 149.8 %shard_map.95 = bf16[8,128,768]{2,1,0:T(8,128)(2,1)} custom-call(bf16[3,8,128,128]{3,2,1,0:T(8,128)(2,1)} %bitcast.57, bf16[16,128,256]{2,1,0:T(8,128)(2,1)} %bitcast.55), custom_call_target="tpu_custom_call" | custom-call | flops 1610612736 | bytes 8388608 | tf_op jit(solution)/shard_map/pallas_call | solution.py:285
  189.1 0.0 all-to-all-done.1
  189.1 0.1 bitcast_convert_fusion
  189.2 0.0 copy-start.2
  189.3 1.0 gather_fusion
  190.2 0.0 copy-done.2
  190.3 1.0 multiply_convert_fusion
  191.2 2.7 %copy.17 = bf16[1024,768]{1,0:T(8,128)(2,1)} copy(bf16[1024,768]{1,0:T(8,128)(2,1)} %bitcast.54) | data formatting | bytes 3145728
  (3 shorter events, 0.0 us)
Async XLA Ops:
  0.6 9.7 %copy-start.3 = (s32[128,1]{0,1:T(1,128)S(1)}, s32[128,1]{0,1:T(1,128)}, u32[]{:S(2)}) copy-start(s32[128,1]{0,1:T(1,128)} %param.9) | copy-start | bytes 1540
  0.6 9.5 %copy-start.5 = (s32[1,64]{1,0:T(1,128)S(1)}, s32[1,64]{1,0:T(1,128)}, u32[]{:S(2)}) copy-start(s32[1,64]{1,0:T(1,128)} %param.15) | copy-start | bytes 772
  5.9 18.7 %all-to-all-start = ((bf16[4,32,4096]{2,1,0:T(8,128)(2,1)}), bf16[4,32,4096]{2,1,0:T(8,128)(2,1)S(1)}, u32[]{:S(2)}, u32[]{:S(2)}) async-start(bf16[4,32,4096]{2,1,0:T(8,128)(2,1)} %bitcast.3), calls=%async_computation | async-start | bytes 2097152 | tf_op jit(solution)/shard_map/all_to_all | solution.py:343
  24.6 3.9 %copy-start.1 = (bf16[1,2048,1024]{2,1,0:T(8,128)(2,1)S(1)}, bf16[1,2048,1024]{2,1,0:T(8,128)(2,1)}, u32[]{:S(2)}) copy-start(bf16[1,2048,1024]{2,1,0:T(8,128)(2,1)} %param.13) | copy-start | bytes 12582916
  24.6 4.7 %copy-start.4 = (bf16[1,2048,1024]{2,1,0:T(8,128)(2,1)S(1)}, bf16[1,2048,1024]{2,1,0:T(8,128)(2,1)}, u32[]{:S(2)}) copy-start(bf16[1,2048,1024]{2,1,0:T(8,128)(2,1)} %param.12) | copy-start | bytes 12582916
  29.3 2.2 %copy-start = (bf16[1,1024,2048]{2,1,0:T(8,128)(2,1)S(1)}, bf16[1,1024,2048]{2,1,0:T(8,128)(2,1)}, u32[]{:S(2)}) copy-start(bf16[1,1024,2048]{2,1,0:T(8,128)(2,1)} %param.14) | copy-start | bytes 12582916
  33.0 156.1 %all-to-all-start.1 = ((bf16[4,32,2048]{2,1,0:T(8,128)(2,1)}), bf16[4,32,2048]{2,1,0:T(8,128)(2,1)S(1)}, u32[]{:S(2)}, u32[]{:S(2)}) async-start(bf16[4,32,2048]{2,1,0:T(8,128)(2,1)} %bitcast.8), calls=%async_computation.1 | async-start | bytes 1048576 | tf_op jit(solution)/shard_map/all_to_all | solution.py:355
  189.2 1.0 copy-start.2

commit v2 on v1

--- a/solution.py
+++ b/solution.py
@@ -10,9 +10,12 @@
 
 EW = 4
 TILE = 16
-PIECES = 8
-AHEAD = 2
+PIECES = 16
+N_B = 3
+AHEAD = 3
+LAG = 2
 B_LAG = 2
+B_EVERY = 4
 F32 = jnp.float32
 BF16 = jnp.bfloat16
 
@@ -25,9 +28,9 @@
 def reduce_kernel(
     n, l_ref, r_ref, out_ref, xsend, xrecv, up, down, own_b, up_b, down_b, xs_b, xr_b,
     xs_sem, xr_sem, us_sem, ur_sem, ds_sem, dr_sem,
-    bus_sem, bur_sem, bds_sem, bdr_sem, bx_sem,
+    bus_sem, bur_sem, bds_sem, bdr_sem, bxs_sem, bxr_sem,
 ):
-    na = PIECES - 1
+    na = PIECES - N_B
     n_rep = 2 * n
     tpc = xsend.shape[2]
     tw = xsend.shape[4]
@@ -40,8 +43,6 @@
     above = {"rep": jnp.minimum(rep + 2, n_rep - 1)}
     below = {"rep": jnp.maximum(rep - 2, 0)}
     last = n - 1
-    b_lag = B_LAG if B_LAG * last < na + last else 1
-
     def part(p, r, j):
         t = r * tpc + j
         mat = t // tpw
@@ -63,14 +64,14 @@
     def down_copy(src, p, d):
         return remote(src.at[p, d], down.at[p, d], ds_sem.at[p, d], dr_sem.at[p, d], below)
 
-    def upb_copy(src, d):
-        return remote(src.at[d], up_b.at[d], bus_sem.at[d], bur_sem.at[d], above)
-
-    def downb_copy(src, d):
-        return remote(src.at[d], down_b.at[d], bds_sem.at[d], bdr_sem.at[d], below)
-
-    def xb_copy():
-        return remote(xs_b, xr_b, bx_sem.at[0], bx_sem.at[1], peer)
+    def upb_copy(src, k, d):
+        return remote(src.at[k, d], up_b.at[k, d], bus_sem.at[k, d], bur_sem.at[k, d], above)
+
+    def downb_copy(src, k, d):
+        return remote(src.at[k, d], down_b.at[k, d], bds_sem.at[k, d], bdr_sem.at[k, d], below)
+
+    def xb_copy(k):
+        return remote(xs_b.at[k], xr_b.at[k], bxs_sem.at[k], bxr_sem.at[k], peer)
 
     barrier = pltpu.get_barrier_semaphore()
     mesh_id = pl.DeviceIdType.MESH
@@ -95,27 +96,26 @@
         lax.fori_loop(0, n, one, 0)
         x_copy(p).start()
 
-    send_x(0)
-
-    def build_b(r, c):
-        for j in range(tpc):
-            own_b[r // 2, r % 2, j] = part(na, r, j).astype(BF16)
-        return c
-
-    lax.fori_loop(0, n_rep, build_b, 0)
-
-    @pl.when(z == 0)
-    def _():
-        for d in range(last, 0, -1):
-            upb_copy(own_b, d).start()
-
-    @pl.when(z == last)
-    def _():
-        for d in range(last):
-            downb_copy(own_b, d).start()
-
-    for p in range(1, AHEAD):
+    for p in range(AHEAD):
         send_x(p)
+
+    def send_b(k):
+        def build_b(r, c):
+            for j in range(tpc):
+                own_b[k, r // 2, r % 2, j] = part(na + k, r, j).astype(BF16)
+            return c
+
+        lax.fori_loop(0, n_rep, build_b, 0)
+
+        @pl.when(z == 0)
+        def _():
+            for d in range(last, 0, -1):
+                upb_copy(own_b, k, d).start()
+
+        @pl.when(z == last)
+        def _():
+            for d in range(last):
+                downb_copy(own_b, k, d).start()
 
     def add_into(dst, src):
         for j in range(tpc):
@@ -125,6 +125,10 @@
         @pl.when(i + AHEAD < na)
         def _():
             send_x(i + AHEAD)
+
+        @pl.when((i % B_EVERY == 0) & (i // B_EVERY < N_B))
+        def _():
+            send_b(i // B_EVERY)
 
         @pl.when(i < na)
         def _():
@@ -147,7 +151,7 @@
                 for d in range(last):
                     down_copy(xrecv, i, d).start()
 
-        q = i - z
+        q = i - LAG * z
 
         @pl.when((z > 0) & (z < last) & (q >= 0) & (q < na))
         def _():
@@ -158,7 +162,7 @@
                     add_into(up.at[q, d], xrecv.at[q, d])
                     up_copy(up, q, d).start()
 
-        w = i - (last - z)
+        w = i - LAG * (last - z)
 
         @pl.when((z > 0) & (z < last) & (w >= 0) & (w < na))
         def _():
@@ -169,7 +173,7 @@
                     add_into(down.at[w, d], xrecv.at[w, d])
                     down_copy(down, w, d).start()
 
-        f = i - last
+        f = i - LAG * last
 
         @pl.when((f >= 0) & (f < na))
         def _():
@@ -187,55 +191,71 @@
                 total += jnp.where(z < last, down[f, z, j].astype(F32), 0.0)
                 out_ref[f, :, j * tw:(j + 1) * tw] = (total / n_rep).astype(BF16)
 
-        @pl.when((z > 0) & (z < last) & (i == b_lag * z))
-        def _():
+        bu = i - B_LAG * z
+
+        @pl.when((z > 0) & (z < last) & (bu >= 0) & (bu % B_EVERY == 0) & (bu // B_EVERY < N_B))
+        def _():
+            k = bu // B_EVERY
             for d in range(last, 1, -1):
                 @pl.when(d > z)
                 def _():
-                    upb_copy(up_b, d).wait_recv()
-                    for k in range(2):
-                        add_into(up_b.at[d, k], own_b.at[d, k])
-                    upb_copy(up_b, d).start()
-
-        @pl.when((z > 0) & (z < last) & (i == b_lag * (last - z)))
-        def _():
+                    upb_copy(up_b, k, d).wait_recv()
+                    for c in range(2):
+                        add_into(up_b.at[k, d, c], own_b.at[k, d, c])
+                    upb_copy(up_b, k, d).start()
+
+        bd = i - B_LAG * (last - z)
+
+        @pl.when((z > 0) & (z < last) & (bd >= 0) & (bd % B_EVERY == 0) & (bd // B_EVERY < N_B))
+        def _():
+            k = bd // B_EVERY
             for d in range(last - 1):
                 @pl.when(d < z)
                 def _():
-                    downb_copy(down_b, d).wait_recv()
-                    for k in range(2):
-                        add_into(down_b.at[d, k], own_b.at[d, k])
-                    downb_copy(down_b, d).start()
-
-        @pl.when(i == b_lag * last)
-        def _():
+                    downb_copy(down_b, k, d).wait_recv()
+                    for c in range(2):
+                        add_into(down_b.at[k, d, c], own_b.at[k, d, c])
+                    downb_copy(down_b, k, d).start()
+
+        bf = i - B_LAG * last
+
+        @pl.when((bf >= 0) & (bf % B_EVERY == 0) & (bf // B_EVERY < N_B))
+        def _():
+            k = bf // B_EVERY
+
             @pl.when(z > 0)
             def _():
-                upb_copy(up_b, z).wait_recv()
+                upb_copy(up_b, k, z).wait_recv()
 
             @pl.when(z < last)
             def _():
-                downb_copy(down_b, z).wait_recv()
-
-            for k in range(2):
-                for j in range(tpc):
-                    total = own_b[z, k, j].astype(F32)
-                    total += jnp.where(z > 0, up_b[z, k, j].astype(F32), 0.0)
-                    total += jnp.where(z < last, down_b[z, k, j].astype(F32), 0.0)
-                    own_b[z, k, j] = total.astype(BF16)
+                downb_copy(down_b, k, z).wait_recv()
+
+            def total(c, j):
+                t = own_b[k, z, c, j].astype(F32)
+                t += jnp.where(z > 0, up_b[k, z, c, j].astype(F32), 0.0)
+                return t + jnp.where(z < last, down_b[k, z, c, j].astype(F32), 0.0)
+
             for j in range(tpc):
-                xs_b[j] = own_b[z, 1 - x, j]
-            xb_copy().start()
+                xs_b[k, j] = total(1 - x, j).astype(BF16)
+            xb_copy(k).start()
+            for j in range(tpc):
+                own_b[k, z, x, j] = total(x, j).astype(BF16)
 
         return carry
 
-    lax.fori_loop(0, na + last, step, 0)
-
-    xb_copy().wait_recv()
-    for j in range(tpc):
-        total = own_b[z, x, j].astype(F32) + xr_b[j].astype(F32)
-        out_ref[na, :, j * tw:(j + 1) * tw] = (total / n_rep).astype(BF16)
-    xb_copy().wait_send()
+    steps = max(na + LAG * last, B_EVERY * (N_B - 1) + B_LAG * last + 1)
+    lax.fori_loop(0, steps, step, 0)
+
+    def finish_b(k, carry):
+        xb_copy(k).wait_recv()
+        for j in range(tpc):
+            total = own_b[k, z, x, j].astype(F32) + xr_b[k, j].astype(F32)
+            out_ref[na + k, :, j * tw:(j + 1) * tw] = (total / n_rep).astype(BF16)
+        xb_copy(k).wait_send()
+        return carry
+
+    lax.fori_loop(0, N_B, finish_b, 0)
 
     def drain(i, carry):
         x_copy(i).wait_send()
@@ -258,19 +278,24 @@
 
     lax.fori_loop(0, na, drain, 0)
 
-    @pl.when(z < last)
-    def _():
-        for d in range(1, n):
-            @pl.when(d > z)
-            def _():
-                upb_copy(up_b, d).wait_send()
-
-    @pl.when(z > 0)
-    def _():
-        for d in range(last):
-            @pl.when(d < z)
-            def _():
-                downb_copy(down_b, d).wait_send()
+    def drain_b(k, carry):
+        @pl.when(z < last)
+        def _():
+            for d in range(1, n):
+                @pl.when(d > z)
+                def _():
+                    upb_copy(up_b, k, d).wait_send()
+
+        @pl.when(z > 0)
+        def _():
+            for d in range(last):
+                @pl.when(d < z)
+                def _():
+                    downb_copy(down_b, k, d).wait_send()
+
+        return carry
+
+    lax.fori_loop(0, N_B, drain_b, 0)
 
 
 def reduce_deltas(left, right, n_rep, columns):
@@ -278,7 +303,7 @@
     pr, depth = left.shape[2:]
     tw = right.shape[2]
     tpc = columns // tw
-    na = PIECES - 1
+    na = PIECES - N_B
     chunk = (tpc, pr, tw)
     dma = pltpu.SemaphoreType.DMA
     vmem = pl.BlockSpec(memory_space=pltpu.VMEM)
@@ -292,22 +317,23 @@
             pltpu.VMEM((na, n) + chunk, BF16),
             pltpu.VMEM((na, n) + chunk, BF16),
             pltpu.VMEM((na, n) + chunk, BF16),
-            pltpu.VMEM((n, 2) + chunk, BF16),
-            pltpu.VMEM((n, 2) + chunk, BF16),
-            pltpu.VMEM((n, 2) + chunk, BF16),
-            pltpu.VMEM(chunk, BF16),
-            pltpu.VMEM(chunk, BF16),
+            pltpu.VMEM((N_B, n, 2) + chunk, BF16),
+            pltpu.VMEM((N_B, n, 2) + chunk, BF16),
+            pltpu.VMEM((N_B, n, 2) + chunk, BF16),
+            pltpu.VMEM((N_B,) + chunk, BF16),
+            pltpu.VMEM((N_B,) + chunk, BF16),
             dma((na,)),
             dma((na,)),
             dma((na, n)),
             dma((na, n)),
             dma((na, n)),
             dma((na, n)),
-            dma((n,)),
-            dma((n,)),
-            dma((n,)),
-            dma((n,)),
-            dma((2,)),
+            dma((N_B, n)),
+            dma((N_B, n)),
+            dma((N_B, n)),
+            dma((N_B, n)),
+            dma((N_B,)),
+            dma((N_B,)),
         ],
         compiler_params=pltpu.CompilerParams(
             collective_id=0, has_side_effects=True, vmem_limit_bytes=56 * 2**20

time: 194 us -> 186 us (0.959)
  Pallas kernels: 150 us -> 142 us
    pallas_call x1, Pallas kernels: 150 us -> 142 us  [reduce_deltas(): pl.pallas_call(functools.partial(reduce_kernel, n), out_shape=jax.ShapeDt...]
  transfers between devices with their start and end apart: 2 -> 2, of which waited for: 1 -> 1; matrix products, arithmetic and copies ran while one was open for 2% -> 2% of each run, Pallas kernels for 77% -> 76%
where the time goes in v2:
time: 186 us
  Pallas kernels  142 us (76%)
  waiting for transfers between devices  14.3 us (8%)
  matrix products  10.5 us (6%)
  local copies, waits for them, and re-layouts  7.77 us (4%)
  starting transfers between devices  7.71 us (4%)
  other arithmetic  3.1 us (2%)
    pallas_call x1, Pallas kernels, reduce_deltas(): pl.pallas_call(functools.partial(reduce_kernel, n), out_shape=jax.ShapeDt...  142 us
    all_to_all x1, waiting for transfers between devices, body(): lax.all_to_all(jnp.repeat(both, shards, axis=0), 'exp', split_axis=0, con...  14.3 us
    all_to_all x1, starting transfers between devices, body(): lax.all_to_all(jnp.repeat(both, shards, axis=0), 'exp', split_axis=0, con...  4.24 us
    unnamed x14, local copies, waits for them, and re-layouts  4.17 us
    dot_general x1, matrix products, body(): lax.dot_general(d_rows, wd, (((1,), (1,)), ((), ())), preferred_element_t...  3.85 us
  transfers between devices with their start and end apart: 2, of which 1 were waited for; matrix products, arithmetic and copies ran while one was open for 2% of the time, Pallas kernels for 76%

profile of v2, /device:TPU:0, one launch (start us, length us, event | category | flops | bytes accessed | tf_op | source)
XLA Modules:
  0.0 185.7 jit_solution(13076281501096244905)
XLA Ops:
  0.6 0.0 copy-start.3
  0.6 0.0 copy-start.5
  0.7 0.9 fusion.11
  1.5 0.7 multiply_add_fusion
  2.2 1.2 multiply_convert_fusion.1
  3.4 2.4 %convolution_convert_fusion = bf16[128,4096]{1,0:T(8,128)(2,1)} fusion(bf16[128,2048]{1,0:T(8,128)(2,1)S(1)} %multiply_convert_fusion.1, bf16[128,2048]{1,0:T(8,128)(2,1)} %param.8, s32[128]{0:T(128)S(1)} %multiply_add_fusion), kind=kOutput, calls=%fused_computation.1 | convolution fusion | flops 136855552 | bytes 2097664 | tf_op jit(solution)/shard_map/dot_general | solution.py:366
  5.9 4.2 %all-to-all-start = ((bf16[4,32,4096]{2,1,0:T(8,128)(2,1)}), bf16[4,32,4096]{2,1,0:T(8,128)(2,1)S(1)}, u32[]{:S(2)}, u32[]{:S(2)}) async-start(bf16[4,32,4096]{2,1,0:T(8,128)(2,1)} %bitcast.3), calls=%async_computation | async-start | bytes 2097152 | tf_op jit(solution)/shard_map/all_to_all | solution.py:369
  10.1 0.0 copy-done.5
  10.1 0.1 broadcast_in_dim.21
  10.2 0.1 convert_element_type.72
  10.3 0.0 copy-done.3
  10.3 14.3 %all-to-all-done = bf16[4,32,4096]{2,1,0:T(8,128)(2,1)S(1)} async-done(((bf16[4,32,4096]{2,1,0:T(8,128)(2,1)}), bf16[4,32,4096]{2,1,0:T(8,128)(2,1)S(1)}, u32[]{:S(2)}, u32[]{:S(2)}) %all-to-all-start) | async-done | bytes 1048608 | tf_op jit(solution)/shard_map/all_to_all | solution.py:369
  24.6 0.0 copy-start.1
  24.6 0.0 copy-start.4
  24.6 3.8 %fusion = f32[128,1024]{1,0:T(8,128)S(1)} fusion(bf16[1,1024,2048]{2,1,0:T(8,128)(2,1)} %param.14, bf16[128,4096]{1,0:T(8,128)(2,1)S(1)} %bitcast.49), kind=kOutput, calls=%fused_computation.2 | convolution fusion | flops 536870912 | bytes 5242880 | tf_op jit(solution)/shard_map/dot_general | solution.py:387
  28.4 0.0 copy-done.1
  28.4 0.7 fusion.4
  29.2 0.1 copy-done.4
  29.3 0.0 copy-start
  29.3 1.0 fusion.20
  30.4 1.1 copy-done
  31.5 1.5 fusion.8
  33.0 3.5 %all-to-all-start.1 = ((bf16[4,32,2048]{2,1,0:T(8,128)(2,1)}), bf16[4,32,2048]{2,1,0:T(8,128)(2,1)S(1)}, u32[]{:S(2)}, u32[]{:S(2)}) async-start(bf16[4,32,2048]{2,1,0:T(8,128)(2,1)} %bitcast.8), calls=%async_computation.1 | async-start | bytes 1048576 | tf_op jit(solution)/shard_map/all_to_all | solution.py:381
  36.5 0.1 fusion.15
  36.6 1.2 copy.11
  37.8 0.2 copy.13
  38.0 1.3 copy.15
  39.3 141.6 %shard_map.95 = bf16[16,64,768]{2,1,0:T(8,128)(2,1)} custom-call(bf16[3,16,64,128]{3,2,1,0:T(8,128)(2,1)} %bitcast.57, bf16[16,128,256]{2,1,0:T(8,128)(2,1)} %bitcast.55), custom_call_target="tpu_custom_call" | custom-call | flops 1610612736 | bytes 8388608 | tf_op jit(solution)/shard_map/pallas_call | solution.py:310
  180.9 0.0 all-to-all-done.1
  180.9 0.1 bitcast_convert_fusion
  181.1 0.0 copy-start.2
  181.1 1.0 gather_fusion
  182.0 0.0 copy-done.2
  182.1 1.0 multiply_convert_fusion
  183.0 2.7 %copy.17 = bf16[1024,768]{1,0:T(8,128)(2,1)} copy(bf16[1024,768]{1,0:T(8,128)(2,1)} %bitcast.54) | data formatting | bytes 3145728
  (3 shorter events, 0.0 us)
Async XLA Ops:
  0.6 9.7 %copy-start.3 = (s32[128,1]{0,1:T(1,128)S(1)}, s32[128,1]{0,1:T(1,128)}, u32[]{:S(2)}) copy-start(s32[128,1]{0,1:T(1,128)} %param.9) | copy-start | bytes 1540
  0.6 9.5 %copy-start.5 = (s32[1,64]{1,0:T(1,128)S(1)}, s32[1,64]{1,0:T(1,128)}, u32[]{:S(2)}) copy-start(s32[1,64]{1,0:T(1,128)} %param.15) | copy-start | bytes 772
  5.9 18.7 %all-to-all-start = ((bf16[4,32,4096]{2,1,0:T(8,128)(2,1)}), bf16[4,32,4096]{2,1,0:T(8,128)(2,1)S(1)}, u32[]{:S(2)}, u32[]{:S(2)}) async-start(bf16[4,32,4096]{2,1,0:T(8,128)(2,1)} %bitcast.3), calls=%async_computation | async-start | bytes 2097152 | tf_op jit(solution)/shard_map/all_to_all | solution.py:369
  24.6 3.9 %copy-start.1 = (bf16[1,2048,1024]{2,1,0:T(8,128)(2,1)S(1)}, bf16[1,2048,1024]{2,1,0:T(8,128)(2,1)}, u32[]{:S(2)}) copy-start(bf16[1,2048,1024]{2,1,0:T(8,128)(2,1)} %param.13) | copy-start | bytes 12582916
  24.6 4.7 %copy-start.4 = (bf16[1,2048,1024]{2,1,0:T(8,128)(2,1)S(1)}, bf16[1,2048,1024]{2,1,0:T(8,128)(2,1)}, u32[]{:S(2)}) copy-start(bf16[1,2048,1024]{2,1,0:T(8,128)(2,1)} %param.12) | copy-start | bytes 12582916
  29.3 2.2 %copy-start = (bf16[1,1024,2048]{2,1,0:T(8,128)(2,1)S(1)}, bf16[1,1024,2048]{2,1,0:T(8,128)(2,1)}, u32[]{:S(2)}) copy-start(bf16[1,1024,2048]{2,1,0:T(8,128)(2,1)} %param.14) | copy-start | bytes 12582916
  33.0 147.9 %all-to-all-start.1 = ((bf16[4,32,2048]{2,1,0:T(8,128)(2,1)}), bf16[4,32,2048]{2,1,0:T(8,128)(2,1)S(1)}, u32[]{:S(2)}, u32[]{:S(2)}) async-start(bf16[4,32,2048]{2,1,0:T(8,128)(2,1)} %bitcast.8), calls=%async_computation.1 | async-start | bytes 1048576 | tf_op jit(solution)/shard_map/all_to_all | solution.py:381
  181.1 1.0 copy-start.2

commit v3 on v2

--- a/solution.py
+++ b/solution.py
@@ -25,8 +25,96 @@
     return s * (1.0 + h * (1.0 - s))
 
 
+def exp_copy(src, dst, send, recv, dev):
+    return pltpu.make_async_remote_copy(
+        src_ref=src, dst_ref=dst, send_sem=send, recv_sem=recv,
+        device_id={"exp": dev}, device_id_type=pl.DeviceIdType.MESH,
+    )
+
+
+def greet_exp(barrier, n_exp):
+    me = lax.axis_index("exp")
+    for k in range(1, n_exp):
+        pl.semaphore_signal(
+            barrier, inc=1, device_id={"exp": (me + k) % n_exp},
+            device_id_type=pl.DeviceIdType.MESH,
+        )
+
+
+def exchange_start(n_exp, group, src, land, send_sem, recv_sem):
+    me = lax.axis_index("exp")
+    for k in range(n_exp - 1, 0, -1):
+        to = (me + k) % n_exp
+        exp_copy(
+            src.at[to // group], land.at[me], send_sem.at[k - 1], recv_sem.at[k - 1], to
+        ).start()
+    land[me] = src[me // group]
+
+
+def exchange_wait(n_exp, src, land, send_sem, recv_sem):
+    me = lax.axis_index("exp")
+    for k in range(n_exp - 1, 0, -1):
+        come = (me + n_exp - k) % n_exp
+        copy = exp_copy(src.at[0], land.at[come], send_sem.at[k - 1], recv_sem.at[k - 1], come)
+        copy.wait_recv()
+        copy.wait_send()
+
+
+def dispatch_kernel(
+    n_exp, tok_ref, cot_ref, gate_ref, place_ref, rows_ref, tiles_ref, buf, land, send_sem, recv_sem
+):
+    width = tok_ref.shape[1]
+    tw = tiles_ref.shape[3]
+    barrier = pltpu.get_barrier_semaphore()
+    greet_exp(barrier, n_exp)
+    dy = (gate_ref[...] * cot_ref[...].astype(F32)).astype(BF16)
+    for e in range(EW):
+        buf[e, :, :width] = jnp.dot(
+            place_ref[e], tok_ref[...], preferred_element_type=F32
+        ).astype(BF16)
+        buf[e, :, width:] = jnp.dot(place_ref[e], dy, preferred_element_type=F32).astype(BF16)
+    pl.semaphore_wait(barrier, n_exp - 1)
+    exchange_start(n_exp, n_exp // EW, buf, land, send_sem, recv_sem)
+    exchange_wait(n_exp, buf, land, send_sem, recv_sem)
+    rows_ref[...] = land[...]
+
+    def one(s, c):
+        for t in range(2 * width // tw):
+            tiles_ref[t, s] = land[s, :, t * tw:(t + 1) * tw]
+        return c
+
+    lax.fori_loop(0, n_exp, one, 0)
+
+
+def dispatch(tokens, cotangent, gate, placer, n_exp, tw):
+    rows, width = tokens.shape
+    cap = rows // EW
+    vmem = pl.BlockSpec(memory_space=pltpu.VMEM)
+    return pl.pallas_call(
+        functools.partial(dispatch_kernel, n_exp),
+        out_shape=(
+            jax.ShapeDtypeStruct((n_exp, cap, 2 * width), BF16),
+            jax.ShapeDtypeStruct((2 * width // tw, n_exp, cap, tw), BF16),
+        ),
+        in_specs=[vmem] * 4,
+        out_specs=(vmem, vmem),
+        scratch_shapes=[
+            pltpu.VMEM((EW, cap, 2 * width), BF16),
+            pltpu.VMEM((n_exp, cap, 2 * width), BF16),
+            pltpu.SemaphoreType.DMA((n_exp - 1,)),
+            pltpu.SemaphoreType.DMA((n_exp - 1,)),
+        ],
+        compiler_params=pltpu.CompilerParams(
+            collective_id=1, has_side_effects=True, vmem_limit_bytes=48 * 2**20
+        ),
+        cost_estimate=pl.CostEstimate(
+            flops=4 * rows * rows * width, bytes_accessed=6 * 2**20, transcendentals=0
+        ),
+    )(tokens, cotangent, gate, placer.reshape(EW, cap, rows))
+
+
 def reduce_kernel(
-    n, l_ref, r_ref, out_ref, xsend, xrecv, up, down, own_b, up_b, down_b, xs_b, xr_b,
+    n, n_exp, l_ref, r_ref, p_ref, out_ref, ret_ref, ret, rs_sem, rr_sem, xsend, xrecv, up, down, own_b, up_b, down_b, xs_b, xr_b,
     xs_sem, xr_sem, us_sem, ur_sem, ds_sem, dr_sem,
     bus_sem, bur_sem, bds_sem, bdr_sem, bxs_sem, bxr_sem,
 ):
@@ -75,6 +163,7 @@
 
     barrier = pltpu.get_barrier_semaphore()
     mesh_id = pl.DeviceIdType.MESH
+    greet_exp(barrier, n_exp)
     pl.semaphore_signal(barrier, inc=1, device_id=peer, device_id_type=mesh_id)
 
     @pl.when(z < last)
@@ -85,7 +174,7 @@
     def _():
         pl.semaphore_signal(barrier, inc=1, device_id=below, device_id_type=mesh_id)
 
-    pl.semaphore_wait(barrier, 1 + jnp.where(z < last, 1, 0) + jnp.where(z > 0, 1, 0))
+    pl.semaphore_wait(barrier, n_exp + jnp.where(z < last, 1, 0) + jnp.where(z > 0, 1, 0))
 
     def send_x(p):
         def one(d, c):
@@ -98,6 +187,7 @@
 
     for p in range(AHEAD):
         send_x(p)
+    exchange_start(n_exp, 1, p_ref, ret, rs_sem, rr_sem)
 
     def send_b(k):
         def build_b(r, c):
@@ -246,6 +336,9 @@
 
     steps = max(na + LAG * last, B_EVERY * (N_B - 1) + B_LAG * last + 1)
     lax.fori_loop(0, steps, step, 0)
+
+    exchange_wait(n_exp, p_ref, ret, rs_sem, rr_sem)
+    ret_ref[...] = ret[...]
 
     def finish_b(k, carry):
         xb_copy(k).wait_recv()
@@ -298,7 +391,7 @@
     lax.fori_loop(0, N_B, drain_b, 0)
 
 
-def reduce_deltas(left, right, n_rep, columns):
+def reduce_deltas(left, right, parts, n_rep, columns):
     n = n_rep // 2
     pr, depth = left.shape[2:]
     tw = right.shape[2]
@@ -307,12 +400,19 @@
     chunk = (tpc, pr, tw)
     dma = pltpu.SemaphoreType.DMA
     vmem = pl.BlockSpec(memory_space=pltpu.VMEM)
-    out = pl.pallas_call(
-        functools.partial(reduce_kernel, n),
-        out_shape=jax.ShapeDtypeStruct((PIECES, pr, columns), BF16),
-        in_specs=[vmem] * 2,
-        out_specs=vmem,
+    n_exp = parts.shape[0]
+    out, returned = pl.pallas_call(
+        functools.partial(reduce_kernel, n, n_exp),
+        out_shape=(
+            jax.ShapeDtypeStruct((PIECES, pr, columns), BF16),
+            jax.ShapeDtypeStruct(parts.shape, BF16),
+        ),
+        in_specs=[vmem] * 3,
+        out_specs=(vmem, vmem),
         scratch_shapes=[
+            pltpu.VMEM(parts.shape, BF16),
+            dma((n_exp - 1,)),
+            dma((n_exp - 1,)),
             pltpu.VMEM((na, n) + chunk, BF16),
             pltpu.VMEM((na, n) + chunk, BF16),
             pltpu.VMEM((na, n) + chunk, BF16),
@@ -342,8 +442,8 @@
             flops=2 * 3 * PIECES * pr * depth * columns * n_rep // 3,
             bytes_accessed=8 * 2**20, transcendentals=0,
         ),
-    )(left, right)
-    return out.reshape(PIECES * pr, columns)
+    )(left, right, parts)
+    return out.reshape(PIECES * pr, columns), returned
 
 
 def body(tokens, expert_ids, gate_prob, cotangent, w_gate, w_up, w_down, touched):
@@ -362,13 +462,11 @@
     slot_of = jnp.sum(onehot * earlier, axis=1).astype(jnp.int32)
     target = expert_ids[:, 0] * cap + slot_of
     placer = (target[None, :] == jnp.arange(EW * cap)[:, None]).astype(jnp.bfloat16)
-    dy = (gate_prob[:, None] * cotangent.astype(jnp.float32)).astype(jnp.bfloat16)
-    both = jnp.dot(
-        placer, jnp.concatenate([tokens, dy], axis=1), preferred_element_type=jnp.float32
-    ).astype(jnp.bfloat16).reshape(EW, cap, 2 * width)
-    recv = lax.all_to_all(
-        jnp.repeat(both, shards, axis=0), "exp", split_axis=0, concat_axis=0, tiled=True
-    ).reshape(n_exp * cap, 2 * width)
+    columns = 3 * width // n_rep
+    tw = math.gcd(columns, width)
+    recv, right = dispatch(tokens, cotangent, gate_prob[:, None], placer, n_exp, tw)
+    recv = recv.reshape(n_exp * cap, 2 * width)
+    right = right.reshape(2 * width // tw, n_exp * cap, tw)
     x_rows = recv[:, :width]
     d_rows = recv[:, width:]
     wg = w_gate[0]
@@ -378,25 +476,21 @@
     u = jnp.dot(x_rows, wu, preferred_element_type=jnp.float32)
     act = (h * jax.nn.sigmoid(h) * u).astype(jnp.bfloat16)
     partial_out = jnp.dot(act, wd, preferred_element_type=jnp.float32).astype(jnp.bfloat16)
-    returned = lax.all_to_all(
-        partial_out.reshape(n_exp, cap, width), "exp", split_axis=0, concat_axis=0, tiled=True
-    )
-    summed = returned.astype(jnp.float32).reshape(EW, shards, cap, width).sum(axis=1)
-    row_out = jnp.take(summed.reshape(EW * cap, width), target, axis=0)
-    mixed = (gate_prob[:, None] * row_out).astype(jnp.bfloat16)
     grad_a = lax.dot_general(
         d_rows, wd, (((1,), (1,)), ((), ())), preferred_element_type=jnp.float32
     )
     d_h = (grad_a * u * swish_slope(h)).astype(jnp.bfloat16)
     d_u = (grad_a * h * jax.nn.sigmoid(h)).astype(jnp.bfloat16)
     hidden = d_h.shape[1]
-    columns = 3 * width // n_rep
-    tw = math.gcd(columns, width)
     mask = jnp.repeat(touched[0], TILE).astype(jnp.bfloat16)
     left = (jnp.stack([d_h, d_u, act]) * mask[None, None, :]).transpose(0, 2, 1)
     left = left.reshape(3, PIECES, hidden // PIECES, left.shape[2])
-    right = recv.reshape(recv.shape[0], 2 * width // tw, tw).transpose(1, 0, 2)
-    averaged = reduce_deltas(left, right, n_rep, columns)
+    averaged, returned = reduce_deltas(
+        left, right, partial_out.reshape(n_exp, cap, width), n_rep, columns
+    )
+    summed = returned.astype(jnp.float32).reshape(EW, shards, cap, width).sum(axis=1)
+    row_out = jnp.take(summed.reshape(EW * cap, width), target, axis=0)
+    mixed = (gate_prob[:, None] * row_out).astype(jnp.bfloat16)
     return (mixed, averaged)
 
 

time: 186 us -> 180 us (0.968)
  Pallas kernels: 142 us -> 157 us
  waiting for transfers between devices: 14.3 us -> 0 us
  starting transfers between devices: 7.71 us -> 0 us
    pallas_call x1 -> x2, Pallas kernels: 142 us -> 157 us  [the longest x1 142 us: reduce_deltas(): pl.pallas_call(functools.partial(reduce_kernel, n, n_exp), out_shape=(jax...]
    all_to_all x2 -> x0, waiting for transfers between devices: 14.3 us -> none  [the longest x1 14.3 us: body(): lax.all_to_all(jnp.repeat(both, shards, axis=0), 'exp', split_axis=0, con...]
    all_to_all x2 -> x0, starting transfers between devices: 7.71 us -> none  [the longest x1 4.24 us: body(): lax.all_to_all(jnp.repeat(both, shards, axis=0), 'exp', split_axis=0, con...]
    dot_general x1 -> x0, matrix products: 2.44 us -> none  [body(): jnp.dot(placer, jnp.concatenate([tokens, dy], axis=1), preferred_element_...]
    dot_general x1, matrix products: 1.04 us -> 3.31 us  [body(): h = jnp.dot(x_rows, wg, preferred_element_type=jnp.float32)]
    dot_general x1, matrix products: 3.85 us -> 1.62 us  [body(): lax.dot_general(d_rows, wd, (((1,), (1,)), ((), ())), preferred_element_t...]
    dot_general x1, matrix products: 1.53 us -> 3.7 us  [body(): jnp.dot(act, wd, preferred_element_type=jnp.float32).astype(jnp.bfloat16)]
    unnamed x14 -> x17, local copies, waits for them, and re-layouts: 4.17 us -> 4.76 us
  transfers between devices with their start and end apart: 2 -> 0, of which waited for: 1 -> 0; matrix products, arithmetic and copies ran while one was open for 2% -> 0% of each run, Pallas kernels for 76% -> 0%
where the time goes in v3:
time: 180 us; the launch traced here: 179 us
  Pallas kernels  157 us (87%)
  matrix products  10.2 us (6%)
  local copies, waits for them, and re-layouts  7.82 us (4%)
  other arithmetic  3 us (2%)
    pallas_call x1, Pallas kernels, reduce_deltas(): pl.pallas_call(functools.partial(reduce_kernel, n, n_exp), out_shape=(jax...  142 us
    pallas_call x1, Pallas kernels, dispatch(): pl.pallas_call(functools.partial(dispatch_kernel, n_exp), out_shape=(jax....  15.8 us
    unnamed x17, local copies, waits for them, and re-layouts  4.76 us
    dot_general x1, matrix products, body(): jnp.dot(act, wd, preferred_element_type=jnp.float32).astype(jnp.bfloat16)  3.7 us

profile of v3, /device:TPU:0, one launch (start us, length us, event | category | flops | bytes accessed | tf_op | source)
XLA Modules:
  0.0 179.3 jit_solution(8241901943633200794)
XLA Ops:
  0.6 0.9 fusion.11
  1.5 0.7 multiply_add_fusion.1
  2.2 0.1 compare_convert_fusion.place_ref
  2.3 0.8 copy.12.gate_ref
  3.0 0.0 copy-start
  3.1 1.0 copy-done
  4.1 0.0 copy-start.1
  4.1 1.0 copy-done.1
  5.1 0.0 copy-start.3
  5.1 15.8 %shard_map.95 = (bf16[4,32,4096]{2,1,0:T(8,128)(2,1)S(1)}, bf16[16,4,32,256]{3,2,1,0:T(8,128)(2,1)S(1)}) custom-call(bf16[128,2048]{1,0:T(8,128)(2,1)S(1)} %copy-done, bf16[128,2048]{1,0:T(8,128)(2,1)S(1)} %copy-done.1, f32[128,1]{1,0:T(8,128)S(1)} %copy.12.gate_ref, bf16[4,32,128]{2,1,0:T(8,128)(2,1)S(1)} %compare_convert_fusion.place_ref), custom_call_target="tpu_custom_call" | custom-call | flops 134217728 | bytes 6291456 | tf_op jit(solution)/shard_map/pallas_call | solution.py:93
  20.9 0.0 copy-start.2
  20.9 0.0 copy-start.4
  21.0 3.3 %fusion = f32[128,1024]{1,0:T(8,128)S(1)} fusion(bf16[1,2048,1024]{2,1,0:T(8,128)(2,1)} %param.12, bf16[128,4096]{1,0:T(8,128)(2,1)S(1)} %bitcast.44), kind=kOutput, calls=%fused_computation.1 | convolution fusion | flops 536870912 | bytes 5242880 | tf_op jit(solution)/shard_map/dot_general | solution.py:475
  24.3 0.0 copy-done.3
  24.3 0.7 fusion.2
  25.0 0.0 copy-done.2
  25.0 0.0 copy-done.4
  25.0 0.0 copy-start.7
  25.0 1.6 fusion.17
  26.7 0.0 copy-done.7
  26.7 0.1 broadcast_in_dim.23
  26.8 0.1 convert_element_type.62
  26.9 0.1 fusion.12
  27.0 1.2 copy.13
  28.1 3.7 %fusion.8 = bf16[128,2048]{1,0:T(8,128)(2,1)} fusion(bf16[128,1024]{1,0:T(8,128)(2,1)S(1)} %get-tuple-element.14, bf16[1,1024,2048]{2,1,0:T(8,128)(2,1)} %param.14), kind=kOutput, calls=%fused_computation.9 | convolution fusion | flops 537133056 | bytes 4980736 | tf_op jit(solution)/shard_map/dot_general | solution.py:478
  31.8 0.0 copy-start.6
  31.8 141.7 %shard_map.96 = (bf16[16,64,768]{2,1,0:T(8,128)(2,1)}, bf16[4,32,2048]{2,1,0:T(8,128)(2,1)}) custom-call(bf16[3,16,64,128]{3,2,1,0:T(8,128)(2,1)} %bitcast.50, bf16[16,128,256]{2,1,0:T(8,128)(2,1)} %bitcast.47, bf16[4,32,2048]{2,1,0:T(8,128)(2,1)} %bitcast.51), custom_call_target="tpu_custom_call" | custom-call | flops 1610612736 | bytes 8388608 | tf_op jit(solution)/shard_map/pallas_call | solution.py:404
  173.5 1.1 bitcast_convert_fusion
  174.7 0.0 copy-done.6
  174.7 0.0 copy-start.5
  174.7 1.0 gather_fusion
  175.7 0.0 copy-done.5
  175.7 1.0 multiply_convert_fusion
  176.7 2.7 %copy.15 = bf16[1024,768]{1,0:T(8,128)(2,1)} copy(bf16[1024,768]{1,0:T(8,128)(2,1)} %bitcast.48) | data formatting | bytes 3145728
  (4 shorter events, 0.0 us)
Async XLA Ops:
  3.0 1.0 copy-start
  4.1 1.0 copy-start.1
  5.1 19.2 %copy-start.3 = (bf16[1,2048,1024]{2,1,0:T(8,128)(2,1)S(1)}, bf16[1,2048,1024]{2,1,0:T(8,128)(2,1)}, u32[]{:S(2)}) copy-start(bf16[1,2048,1024]{2,1,0:T(8,128)(2,1)} %param.13) | copy-start | bytes 12582916
  20.9 4.1 %copy-start.2 = (bf16[16,4,32,256]{3,2,1,0:T(8,128)(2,1)}, bf16[16,4,32,256]{3,2,1,0:T(8,128)(2,1)S(1)}, u32[]{:S(2)}) copy-start(bf16[16,4,32,256]{3,2,1,0:T(8,128)(2,1)S(1)} %get-tuple-element.7) | copy-start | bytes 3145732
  20.9 4.1 %copy-start.4 = (bf16[1,1024,2048]{2,1,0:T(8,128)(2,1)S(1)}, bf16[1,1024,2048]{2,1,0:T(8,128)(2,1)}, u32[]{:S(2)}) copy-start(bf16[1,1024,2048]{2,1,0:T(8,128)(2,1)} %param.14) | copy-start | bytes 12582916
  25.0 1.6 copy-start.7
  31.8 142.8 %copy-start.6 = (s32[128,1]{0,1:T(1,128)S(1)}, s32[128,1]{0,1:T(1,128)}, u32[]{:S(2)}) copy-start(s32[128,1]{0,1:T(1,128)} %param.9) | copy-start | bytes 1540
  174.7 1.0 copy-start.5

commit v4 on v3

--- a/solution.py
+++ b/solution.py
@@ -114,7 +114,7 @@
 
 
 def reduce_kernel(
-    n, n_exp, l_ref, r_ref, p_ref, out_ref, ret_ref, ret, rs_sem, rr_sem, xsend, xrecv, up, down, own_b, up_b, down_b, xs_b, xr_b,
+    n, n_exp, l_ref, r_ref, p_ref, home_ref, gate_ref, out_ref, mix_ref, ret, rs_sem, rr_sem, xsend, xrecv, up, down, own_b, up_b, down_b, xs_b, xr_b,
     xs_sem, xr_sem, us_sem, ur_sem, ds_sem, dr_sem,
     bus_sem, bur_sem, bds_sem, bdr_sem, bxs_sem, bxr_sem,
 ):
@@ -185,38 +185,60 @@
         lax.fori_loop(0, n, one, 0)
         x_copy(p).start()
 
+    def send_b(k):
+        def one(m, c):
+            d = jnp.where(z == 0, last - m, m)
+
+            def build(xi, c):
+                for j in range(tpc):
+                    own_b[k, d, xi, j] = part(na + k, 2 * d + xi, j).astype(BF16)
+                return c
+
+            lax.fori_loop(0, 2, build, 0)
+
+            @pl.when((z == 0) & (m < last))
+            def _():
+                upb_copy(own_b, k, d).start()
+
+            @pl.when((z == last) & (m < last))
+            def _():
+                downb_copy(own_b, k, d).start()
+
+            return c
+
+        lax.fori_loop(0, n, one, 0)
+
+    send_b(0)
     for p in range(AHEAD):
         send_x(p)
     exchange_start(n_exp, 1, p_ref, ret, rs_sem, rr_sem)
 
-    def send_b(k):
-        def build_b(r, c):
-            for j in range(tpc):
-                own_b[k, r // 2, r % 2, j] = part(na + k, r, j).astype(BF16)
-            return c
-
-        lax.fori_loop(0, n_rep, build_b, 0)
-
-        @pl.when(z == 0)
-        def _():
-            for d in range(last, 0, -1):
-                upb_copy(own_b, k, d).start()
-
-        @pl.when(z == last)
-        def _():
-            for d in range(last):
-                downb_copy(own_b, k, d).start()
-
     def add_into(dst, src):
         for j in range(tpc):
             dst[j] = (dst[j].astype(F32) + src[j].astype(F32)).astype(BF16)
 
+    def combine():
+        width = ret.shape[2]
+        cw = math.gcd(width, 512)
+        for c in range(0, width, cw):
+            rows = jnp.zeros((mix_ref.shape[0], cw), F32)
+            for s in range(n_exp):
+                rows += jnp.dot(
+                    home_ref[s * EW // n_exp], ret[s, :, c:c + cw], preferred_element_type=F32
+                )
+            mix_ref[:, c:c + cw] = (gate_ref[...] * rows).astype(BF16)
+
     def step(i, carry):
+        @pl.when(i == na)
+        def _():
+            exchange_wait(n_exp, p_ref, ret, rs_sem, rr_sem)
+            combine()
+
         @pl.when(i + AHEAD < na)
         def _():
             send_x(i + AHEAD)
 
-        @pl.when((i % B_EVERY == 0) & (i // B_EVERY < N_B))
+        @pl.when((i > 0) & (i % B_EVERY == 0) & (i // B_EVERY < N_B))
         def _():
             send_b(i // B_EVERY)
 
@@ -336,9 +358,6 @@
 
     steps = max(na + LAG * last, B_EVERY * (N_B - 1) + B_LAG * last + 1)
     lax.fori_loop(0, steps, step, 0)
-
-    exchange_wait(n_exp, p_ref, ret, rs_sem, rr_sem)
-    ret_ref[...] = ret[...]
 
     def finish_b(k, carry):
         xb_copy(k).wait_recv()
@@ -391,7 +410,7 @@
     lax.fori_loop(0, N_B, drain_b, 0)
 
 
-def reduce_deltas(left, right, parts, n_rep, columns):
+def reduce_deltas(left, right, parts, home, gate, n_rep, columns):
     n = n_rep // 2
     pr, depth = left.shape[2:]
     tw = right.shape[2]
@@ -401,13 +420,13 @@
     dma = pltpu.SemaphoreType.DMA
     vmem = pl.BlockSpec(memory_space=pltpu.VMEM)
     n_exp = parts.shape[0]
-    out, returned = pl.pallas_call(
+    out, mixed = pl.pallas_call(
         functools.partial(reduce_kernel, n, n_exp),
         out_shape=(
             jax.ShapeDtypeStruct((PIECES, pr, columns), BF16),
-            jax.ShapeDtypeStruct(parts.shape, BF16),
-        ),
-        in_specs=[vmem] * 3,
+            jax.ShapeDtypeStruct((gate.shape[0], parts.shape[2]), BF16),
+        ),
+        in_specs=[vmem] * 5,
         out_specs=(vmem, vmem),
         scratch_shapes=[
             pltpu.VMEM(parts.shape, BF16),
@@ -442,8 +461,8 @@
             flops=2 * 3 * PIECES * pr * depth * columns * n_rep // 3,
             bytes_accessed=8 * 2**20, transcendentals=0,
         ),
-    )(left, right, parts)
-    return out.reshape(PIECES * pr, columns), returned
+    )(left, right, parts, home, gate)
+    return out.reshape(PIECES * pr, columns), mixed
 
 
 def body(tokens, expert_ids, gate_prob, cotangent, w_gate, w_up, w_down, touched):
@@ -451,7 +470,6 @@
     width = tokens.shape[1]
     n_exp = lax.axis_size("exp")
     n_rep = lax.axis_size("rep")
-    shards = n_exp // EW
     cap = rows // EW
     onehot = (expert_ids == jnp.arange(EW)[None, :]).astype(jnp.float32)
     lower = (
@@ -485,12 +503,13 @@
     mask = jnp.repeat(touched[0], TILE).astype(jnp.bfloat16)
     left = (jnp.stack([d_h, d_u, act]) * mask[None, None, :]).transpose(0, 2, 1)
     left = left.reshape(3, PIECES, hidden // PIECES, left.shape[2])
-    averaged, returned = reduce_deltas(
-        left, right, partial_out.reshape(n_exp, cap, width), n_rep, columns
+    home = (
+        target[None, :, None] == jnp.arange(EW * cap).reshape(EW, 1, cap)
+    ).astype(jnp.bfloat16)
+    averaged, mixed = reduce_deltas(
+        left, right, partial_out.reshape(n_exp, cap, width), home, gate_prob[:, None],
+        n_rep, columns,
     )
-    summed = returned.astype(jnp.float32).reshape(EW, shards, cap, width).sum(axis=1)
-    row_out = jnp.take(summed.reshape(EW * cap, width), target, axis=0)
-    mixed = (gate_prob[:, None] * row_out).astype(jnp.bfloat16)
     return (mixed, averaged)
 
 

time: 180 us -> 181 us (level)
  Pallas kernels: 157 us -> 159 us
    unnamed x17 -> x14, local copies, waits for them, and re-layouts: 4.76 us -> 6.63 us
where the time goes in v4:
time: 181 us
  Pallas kernels  159 us (88%)
  matrix products  10.2 us (6%)
  local copies, waits for them, and re-layouts  8.73 us (5%)
  other arithmetic  2.28 us (1%)
    pallas_call x1, Pallas kernels, reduce_deltas(): pl.pallas_call(functools.partial(reduce_kernel, n, n_exp), out_shape=(jax...  143 us
    pallas_call x1, Pallas kernels, dispatch(): pl.pallas_call(functools.partial(dispatch_kernel, n_exp), out_shape=(jax....  15.8 us
    unnamed x14, local copies, waits for them, and re-layouts  6.63 us
    dot_general x1, matrix products, body(): jnp.dot(act, wd, preferred_element_type=jnp.float32).astype(jnp.bfloat16)  3.7 us

profile of v4, /device:TPU:0, one launch (start us, length us, event | category | flops | bytes accessed | tf_op | source)
XLA Modules:
  0.0 181.0 jit_solution(10814743555148995226)
XLA Ops:
  0.6 0.7 convert_bitcast_fusion
  1.3 0.9 fusion.11
  2.2 0.7 convert_add_fusion
  2.9 0.1 broadcast_in_dim.5
  2.9 0.1 convert_element_type.53
  3.0 0.1 compare_convert_fusion.1.place_ref
  3.1 0.8 copy.13.gate_ref
  3.9 0.0 copy-start.2
  3.9 0.7 compare_convert_fusion.home_ref
  4.6 0.0 copy-start
  4.6 1.0 copy-done
  5.7 0.0 copy-start.1
  5.7 1.0 copy-done.1
  6.7 0.0 copy-start.4
  6.7 15.8 %shard_map.95 = (bf16[4,32,4096]{2,1,0:T(8,128)(2,1)S(1)}, bf16[16,4,32,256]{3,2,1,0:T(8,128)(2,1)S(1)}) custom-call(bf16[128,2048]{1,0:T(8,128)(2,1)S(1)} %copy-done, bf16[128,2048]{1,0:T(8,128)(2,1)S(1)} %copy-done.1, f32[128,1]{1,0:T(8,128)S(1)} %copy.13.gate_ref, bf16[4,32,128]{2,1,0:T(8,128)(2,1)S(1)} %compare_convert_fusion.1.place_ref), custom_call_target="tpu_custom_call" | custom-call | flops 134217728 | bytes 6291456 | tf_op jit(solution)/shard_map/pallas_call | solution.py:93
  22.5 0.0 copy-start.3
  22.5 0.0 copy-start.5
  22.5 3.3 %fusion = f32[128,1024]{1,0:T(8,128)S(1)} fusion(bf16[1,2048,1024]{2,1,0:T(8,128)(2,1)} %param.12, bf16[128,4096]{1,0:T(8,128)(2,1)S(1)} %bitcast.33), kind=kOutput, calls=%fused_computation | convolution fusion | flops 536870912 | bytes 5242880 | tf_op jit(solution)/shard_map/dot_general | solution.py:493
  25.9 0.0 copy-done.4
  25.9 0.7 fusion.2
  26.6 0.0 copy-done.2
  26.6 0.0 copy-done.3
  26.6 0.0 copy-done.5
  26.6 1.6 fusion.17
  28.3 0.1 fusion.12
  28.4 1.2 copy.14
  29.5 3.7 %fusion.8 = bf16[128,2048]{1,0:T(8,128)(2,1)} fusion(bf16[128,1024]{1,0:T(8,128)(2,1)S(1)} %get-tuple-element.12, bf16[1,1024,2048]{2,1,0:T(8,128)(2,1)} %param.14), kind=kOutput, calls=%fused_computation.8 | convolution fusion | flops 537133056 | bytes 4980736 | tf_op jit(solution)/shard_map/dot_general | solution.py:496
  33.2 143.2 %shard_map.96 = (bf16[16,64,768]{2,1,0:T(8,128)(2,1)}, bf16[128,2048]{1,0:T(8,128)(2,1)}) custom-call(bf16[3,16,64,128]{3,2,1,0:T(8,128)(2,1)} %bitcast.39, bf16[16,128,256]{2,1,0:T(8,128)(2,1)} %bitcast.36, bf16[4,32,2048]{2,1,0:T(8,128)(2,1)} %bitcast.40, bf16[4,128,32]{2,1,0:T(8,128)(2,1)} %compare_convert_fusion.home_ref, f32[128,1]{1,0:T(8,128)} %copy-done.2), custom_call_target="tpu_custom_call" | custom-call | flops 1610612736 | bytes 8388608 | tf_op jit(solution)/shard_map/pallas_call | solution.py:423
  176.5 1.9 %copy.18 = bf16[128,2048]{1,0:T(8,128)(2,1)} copy(bf16[128,2048]{1,0:T(8,128)(2,1)} %get-tuple-element.15) | data formatting | bytes 1048576
  178.3 2.7 %copy.19 = bf16[1024,768]{1,0:T(8,128)(2,1)} copy(bf16[1024,768]{1,0:T(8,128)(2,1)} %bitcast.37) | data formatting | bytes 3145728
  (1 shorter events, 0.0 us)
Async XLA Ops:
  3.9 22.7 %copy-start.2 = (f32[128,1]{1,0:T(8,128)}, f32[128,1]{1,0:T(8,128)S(1)}, u32[]{:S(2)}) copy-start(f32[128,1]{1,0:T(8,128)S(1)} %copy.13.gate_ref) | copy-start | bytes 1540
  4.6 1.0 copy-start
  5.7 1.0 copy-start.1
  6.7 19.2 %copy-start.4 = (bf16[1,2048,1024]{2,1,0:T(8,128)(2,1)S(1)}, bf16[1,2048,1024]{2,1,0:T(8,128)(2,1)}, u32[]{:S(2)}) copy-start(bf16[1,2048,1024]{2,1,0:T(8,128)(2,1)} %param.13) | copy-start | bytes 12582916
  22.5 4.1 %copy-start.3 = (bf16[16,4,32,256]{3,2,1,0:T(8,128)(2,1)}, bf16[16,4,32,256]{3,2,1,0:T(8,128)(2,1)S(1)}, u32[]{:S(2)}) copy-start(bf16[16,4,32,256]{3,2,1,0:T(8,128)(2,1)S(1)} %get-tuple-element.7) | copy-start | bytes 3145732
  22.5 4.1 %copy-start.5 = (bf16[1,1024,2048]{2,1,0:T(8,128)(2,1)S(1)}, bf16[1,1024,2048]{2,1,0:T(8,128)(2,1)}, u32[]{:S(2)}) copy-start(bf16[1,1024,2048]{2,1,0:T(8,128)(2,1)} %param.14) | copy-start | bytes 12582916

commit v5 on v4

--- a/solution.py
+++ b/solution.py
@@ -12,7 +12,7 @@
 TILE = 16
 PIECES = 16
 N_B = 3
-AHEAD = 3
+AHEAD = 4
 LAG = 2
 B_LAG = 2
 B_EVERY = 4
@@ -208,8 +208,9 @@
 
         lax.fori_loop(0, n, one, 0)
 
+    send_x(0)
     send_b(0)
-    for p in range(AHEAD):
+    for p in range(1, AHEAD):
         send_x(p)
     exchange_start(n_exp, 1, p_ref, ret, rs_sem, rr_sem)
 
@@ -229,7 +230,7 @@
             mix_ref[:, c:c + cw] = (gate_ref[...] * rows).astype(BF16)
 
     def step(i, carry):
-        @pl.when(i == na)
+        @pl.when(i == na // 2)
         def _():
             exchange_wait(n_exp, p_ref, ret, rs_sem, rr_sem)
             combine()

time: 181 us -> 180 us (level)
  Pallas kernels: 159 us -> 157 us
where the time goes in v5:
time: 180 us; the launch traced here: 179 us
  Pallas kernels  157 us (87%)
  matrix products  10.2 us (6%)
  local copies, waits for them, and re-layouts  8.73 us (5%)
  other arithmetic  2.28 us (1%)
    pallas_call x1, Pallas kernels, reduce_deltas(): pl.pallas_call(functools.partial(reduce_kernel, n, n_exp), out_shape=(jax...  142 us
    pallas_call x1, Pallas kernels, dispatch(): pl.pallas_call(functools.partial(dispatch_kernel, n_exp), out_shape=(jax....  15.8 us
    unnamed x14, local copies, waits for them, and re-layouts  6.63 us
    dot_general x1, matrix products, body(): jnp.dot(act, wd, preferred_element_type=jnp.float32).astype(jnp.bfloat16)  3.7 us

profile of v5, /device:TPU:0, one launch (start us, length us, event | category | flops | bytes accessed | tf_op | source)
XLA Modules:
  0.0 179.5 jit_solution(1394086781729082002)
XLA Ops:
  0.6 0.7 convert_bitcast_fusion
  1.3 0.9 fusion.11
  2.2 0.7 convert_add_fusion
  2.9 0.1 broadcast_in_dim.5
  2.9 0.1 convert_element_type.53
  3.0 0.1 compare_convert_fusion.1.place_ref
  3.1 0.8 copy.13.gate_ref
  3.9 0.0 copy-start.2
  3.9 0.7 compare_convert_fusion.home_ref
  4.6 0.0 copy-start
  4.6 1.0 copy-done
  5.7 0.0 copy-start.1
  5.7 1.0 copy-done.1
  6.7 0.0 copy-start.4
  6.7 15.8 %shard_map.95 = (bf16[4,32,4096]{2,1,0:T(8,128)(2,1)S(1)}, bf16[16,4,32,256]{3,2,1,0:T(8,128)(2,1)S(1)}) custom-call(bf16[128,2048]{1,0:T(8,128)(2,1)S(1)} %copy-done, bf16[128,2048]{1,0:T(8,128)(2,1)S(1)} %copy-done.1, f32[128,1]{1,0:T(8,128)S(1)} %copy.13.gate_ref, bf16[4,32,128]{2,1,0:T(8,128)(2,1)S(1)} %compare_convert_fusion.1.place_ref), custom_call_target="tpu_custom_call" | custom-call | flops 134217728 | bytes 6291456 | tf_op jit(solution)/shard_map/pallas_call | solution.py:93
  22.5 0.0 copy-start.3
  22.5 0.0 copy-start.5
  22.5 3.3 %fusion = f32[128,1024]{1,0:T(8,128)S(1)} fusion(bf16[1,2048,1024]{2,1,0:T(8,128)(2,1)} %param.12, bf16[128,4096]{1,0:T(8,128)(2,1)S(1)} %bitcast.33), kind=kOutput, calls=%fused_computation | convolution fusion | flops 536870912 | bytes 5242880 | tf_op jit(solution)/shard_map/dot_general | solution.py:494
  25.9 0.0 copy-done.4
  25.9 0.7 fusion.2
  26.6 0.0 copy-done.2
  26.6 0.0 copy-done.3
  26.6 0.0 copy-done.5
  26.6 1.6 fusion.17
  28.3 0.1 fusion.12
  28.4 1.2 copy.14
  29.5 3.7 %fusion.8 = bf16[128,2048]{1,0:T(8,128)(2,1)} fusion(bf16[128,1024]{1,0:T(8,128)(2,1)S(1)} %get-tuple-element.12, bf16[1,1024,2048]{2,1,0:T(8,128)(2,1)} %param.14), kind=kOutput, calls=%fused_computation.8 | convolution fusion | flops 537133056 | bytes 4980736 | tf_op jit(solution)/shard_map/dot_general | solution.py:497
  33.2 141.7 %shard_map.96 = (bf16[16,64,768]{2,1,0:T(8,128)(2,1)}, bf16[128,2048]{1,0:T(8,128)(2,1)}) custom-call(bf16[3,16,64,128]{3,2,1,0:T(8,128)(2,1)} %bitcast.39, bf16[16,128,256]{2,1,0:T(8,128)(2,1)} %bitcast.36, bf16[4,32,2048]{2,1,0:T(8,128)(2,1)} %bitcast.40, bf16[4,128,32]{2,1,0:T(8,128)(2,1)} %compare_convert_fusion.home_ref, f32[128,1]{1,0:T(8,128)} %copy-done.2), custom_call_target="tpu_custom_call" | custom-call | flops 1610612736 | bytes 8388608 | tf_op jit(solution)/shard_map/pallas_call | solution.py:424
  174.9 1.9 %copy.18 = bf16[128,2048]{1,0:T(8,128)(2,1)} copy(bf16[128,2048]{1,0:T(8,128)(2,1)} %get-tuple-element.15) | data formatting | bytes 1048576
  176.8 2.7 %copy.19 = bf16[1024,768]{1,0:T(8,128)(2,1)} copy(bf16[1024,768]{1,0:T(8,128)(2,1)} %bitcast.37) | data formatting | bytes 3145728
  (1 shorter events, 0.0 us)
Async XLA Ops:
  3.9 22.7 %copy-start.2 = (f32[128,1]{1,0:T(8,128)}, f32[128,1]{1,0:T(8,128)S(1)}, u32[]{:S(2)}) copy-start(f32[128,1]{1,0:T(8,128)S(1)} %copy.13.gate_ref) | copy-start | bytes 1540
  4.6 1.0 copy-start
  5.7 1.0 copy-start.1
  6.7 19.2 %copy-start.4 = (bf16[1,2048,1024]{2,1,0:T(8,128)(2,1)S(1)}, bf16[1,2048,1024]{2,1,0:T(8,128)(2,1)}, u32[]{:S(2)}) copy-start(bf16[1,2048,1024]{2,1,0:T(8,128)(2,1)} %param.13) | copy-start | bytes 12582916
  22.5 4.1 %copy-start.3 = (bf16[16,4,32,256]{3,2,1,0:T(8,128)(2,1)}, bf16[16,4,32,256]{3,2,1,0:T(8,128)(2,1)S(1)}, u32[]{:S(2)}) copy-start(bf16[16,4,32,256]{3,2,1,0:T(8,128)(2,1)S(1)} %get-tuple-element.7) | copy-start | bytes 3145732
  22.5 4.1 %copy-start.5 = (bf16[1,1024,2048]{2,1,0:T(8,128)(2,1)S(1)}, bf16[1,1024,2048]{2,1,0:T(8,128)(2,1)}, u32[]{:S(2)}) copy-start(bf16[1,1024,2048]{2,1,0:T(8,128)(2,1)} %param.14) | copy-start | bytes 12582916
